TPU v7x, 512 devices: a whole 4x4x16 slice. The times are simulated.
512 devices in a mesh: slab: 256 (over x, z, y), rhs: 2 (over core).
Axes of the slice: x: 4, y: 4, z: 16, core: 2. Of those that a mesh axis runs over, the one named last changes fastest.
Arguments:
- right_spike: float32 [262144, 256], P('slab'), may hold values from -1.1 to 1.1
- left_spike: float32 [262144, 256], P('slab'), may hold values from -1.1 to 1.1
- local_rhs: float32 [64, 262144], P('rhs', 'slab'), may hold values from -2 to 2
Outputs:
- solution: float32 [64, 262144], P('rhs', 'slab')
All inputs are finite; a program needn't handle non-finite values.
Results may differ from a plain program's by a relative error of at most 0.0001.
Values sent between devices are 32-bit elements; how exact they have to be, the bound alone decides.
A program may use at most 64 MiB of HBM per device.

v0:
```python
import jax
import jax.numpy as jnp
from jax import lax
from jax.sharding import PartitionSpec as P


def swapped(shard, axis, bit):
    return lax.ppermute(shard, axis, [(i, i ^ 1 << bit) for i in range(lax.axis_size(axis))])


def product(left, right):
    return jnp.dot(left, right, precision=lax.Precision.HIGHEST, preferred_element_type=jnp.float32)


def against(rows_in, matrix):
    return lax.dot_general(
        rows_in,
        matrix,
        (((1,), (1,)), ((), ())),
        precision=lax.Precision.HIGHEST,
        preferred_element_type=jnp.float32,
    )


def invert(near_bottom, near_top):
    identity = jnp.eye(near_bottom.shape[0], dtype=jnp.float32)
    coupling = product(near_bottom, near_top)
    kernel = identity - coupling
    approx = identity + coupling
    for sweep_index in range(3):
        approx = product(approx, 2.0 * identity - product(kernel, approx))
    return approx


def local(right_spike, left_spike, local_rhs):
    block_size = right_spike.shape[1]
    part_rows = right_spike.shape[0]
    columns = local_rhs.shape[0]
    levels = lax.axis_size("slab").bit_length() - 1
    position = lax.axis_index("slab")
    core_index = lax.axis_index("rhs")
    far_right = right_spike[:block_size]
    near_right = right_spike[part_rows - block_size :]
    near_left = left_spike[:block_size]
    far_left = left_spike[part_rows - block_size :]
    source_top = local_rhs[:, :block_size]
    source_bottom = local_rhs[:, part_rows - block_size :]
    records = []
    for section_index in range(levels):
        distance = 2**section_index
        in_right = position // distance % 2 == 1
        is_top = section_index == levels - 1
        if is_top:
            spikes_out = jnp.where(in_right, near_left, near_right)
        else:
            spikes_out = jnp.concatenate([far_right, near_right, near_left, far_left], axis=1)
        sources_out = jnp.concatenate([source_top, source_bottom], axis=1)
        packed = jnp.concatenate([spikes_out.reshape(-1), sources_out.reshape(-1)])
        arrived = swapped(packed, "slab", section_index)
        spikes_in = arrived[: spikes_out.size].reshape(spikes_out.shape)
        sources_in = arrived[spikes_out.size :].reshape(sources_out.shape)
        if is_top:
            a_near_right = jnp.where(in_right, spikes_in, near_right)
            b_near_left = jnp.where(in_right, near_left, spikes_in)
        else:
            other_far_right = spikes_in[:, :block_size]
            other_near_right = spikes_in[:, block_size : 2 * block_size]
            other_near_left = spikes_in[:, 2 * block_size : 3 * block_size]
            other_far_left = spikes_in[:, 3 * block_size :]
            a_far_right = jnp.where(in_right, other_far_right, far_right)
            a_near_right = jnp.where(in_right, other_near_right, near_right)
            a_near_left = jnp.where(in_right, other_near_left, near_left)
            a_far_left = jnp.where(in_right, other_far_left, far_left)
            b_far_right = jnp.where(in_right, far_right, other_far_right)
            b_near_right = jnp.where(in_right, near_right, other_near_right)
            b_near_left = jnp.where(in_right, near_left, other_near_left)
            b_far_left = jnp.where(in_right, far_left, other_far_left)
        inverse = invert(a_near_right, b_near_left)
        if not is_top:
            coupled = -product(a_near_right, b_far_right)
            own_solved = product(inverse, jnp.where(core_index == 0, coupled, a_far_left))
            theirs = swapped(own_solved, "rhs", 0)
            right_weight = jnp.where(core_index == 0, own_solved, theirs)
            left_weight = jnp.where(core_index == 0, theirs, own_solved)
            next_right = b_far_right - product(b_near_left, right_weight)
            next_left = product(b_near_left, left_weight)
            far_right = -product(a_far_right, next_right)
            near_right = b_near_right - product(b_far_left, right_weight)
            near_left = a_near_left + product(a_far_right, next_left)
            far_left = -product(b_far_left, left_weight)
        a_top = jnp.where(in_right, sources_in[:, :block_size], source_top)
        a_bottom = jnp.where(in_right, sources_in[:, block_size:], source_bottom)
        b_top = jnp.where(in_right, source_top, sources_in[:, :block_size])
        b_bottom = jnp.where(in_right, source_bottom, sources_in[:, block_size:])
        target = a_bottom - against(b_top, a_near_right)
        middle_source = against(target, inverse)
        next_source = b_top - against(middle_source, b_near_left)
        if is_top:
            records.append((middle_source, next_source))
        else:
            records.append(
                (middle_source, next_source, right_weight, left_weight, next_right, next_left)
            )
            source_top = a_top - against(next_source, a_far_right)
            source_bottom = b_bottom - against(middle_source, b_far_left)
    left_edge = jnp.zeros((columns, block_size), jnp.float32)
    right_edge = jnp.zeros((columns, block_size), jnp.float32)
    for section_index in reversed(range(levels)):
        distance = 2**section_index
        in_right = position // distance % 2 == 1
        record = records[section_index]
        if section_index == levels - 1:
            middle_left = record[0]
            middle_right = record[1]
        else:
            middle_source, next_source, right_weight, left_weight, next_right, next_left = record
            middle_left = (
                middle_source - against(right_edge, right_weight) - against(left_edge, left_weight)
            )
            middle_right = (
                next_source - against(right_edge, next_right) + against(left_edge, next_left)
            )
        left_edge = jnp.where(in_right, middle_left, left_edge)
        right_edge = jnp.where(in_right, right_edge, middle_right)
    return local_rhs - against(right_edge, right_spike) - against(left_edge, left_spike)


def solution(mesh):
    return jax.shard_map(
        local,
        mesh=mesh,
        in_specs=(P("slab", None), P("slab", None), P("rhs", "slab")),
        out_specs=P("rhs", "slab"),
        check_vma=False,
    )
```

profile of v0, /device:TPU:138, one launch (start us, length us, event | category | flops | bytes accessed | tf_op | source)
XLA Modules:
  0.0 527.6 jit_solution(13437761832041074778)
XLA Ops:
  0.8 1.3 fusion.95
  3.5 2.3 collective-permute-start
  5.9 26.0 %collective-permute-done = f32[278528]{0:T(1024)S(1)} collective-permute-done((f32[278528]{0:T(1024)}, f32[278528]{0:T(1024)S(1)}, u32[]{:S(2)}, u32[]{:S(2)}) %collective-permute-start) | collective-permute-done | bytes 1114144 | tf_op jit(solution)/shard_map/ppermute | solution.py:8
  38.9 1.9 collective-permute-start.1
  46.7 4.4 collective-permute-start.2
  51.1 25.8 %collective-permute-done.2 = f32[278528]{0:T(1024)S(1)} collective-permute-done((f32[278528]{0:T(1024)}, f32[278528]{0:T(1024)S(1)}, u32[]{:S(2)}, u32[]{:S(2)}) %collective-permute-start.2) | collective-permute-done | bytes 1114144 | tf_op jit(solution)/shard_map/ppermute | solution.py:8
  79.0 1.4 slice.389
  87.6 1.9 collective-permute-start.3
  96.1 4.1 collective-permute-start.4
  100.2 24.8 %collective-permute-done.4 = f32[278528]{0:T(1024)S(1)} collective-permute-done((f32[278528]{0:T(1024)}, f32[278528]{0:T(1024)S(1)}, u32[]{:S(2)}, u32[]{:S(2)}) %collective-permute-start.4) | collective-permute-done | bytes 1114144 | tf_op jit(solution)/shard_map/ppermute | solution.py:8
  127.1 1.4 slice.399
  135.7 1.9 collective-permute-start.5
  144.2 5.6 %collective-permute-start.6 = (f32[278528]{0:T(1024)}, f32[278528]{0:T(1024)S(1)}, u32[]{:S(2)}, u32[]{:S(2)}) collective-permute-start(f32[278528]{0:T(1024)} %pad_maximum_fusion.3), channel_id=1, source_target_pairs={{0,16},{2,18},{4,20},{6,22},{8,24},{10,26},{12,28},{14,30},{16,0},... | collective-permute-start | bytes 3342344 | tf_op jit(solution)/shard_map/ppermute | solution.py:8
  149.9 48.4 %collective-permute-done.6 = f32[278528]{0:T(1024)S(1)} collective-permute-done((f32[278528]{0:T(1024)}, f32[278528]{0:T(1024)S(1)}, u32[]{:S(2)}, u32[]{:S(2)}) %collective-permute-start.6) | collective-permute-done | bytes 1114144 | tf_op jit(solution)/shard_map/ppermute | solution.py:8
  200.4 1.4 slice.409
  209.1 1.9 collective-permute-start.7
  217.5 2.1 collective-permute-start.8
  219.6 95.3 %collective-permute-done.8 = f32[278528]{0:T(1024)S(1)} collective-permute-done((f32[278528]{0:T(1024)}, f32[278528]{0:T(1024)S(1)}, u32[]{:S(2)}, u32[]{:S(2)}) %collective-permute-start.8) | collective-permute-done | bytes 1114144 | tf_op jit(solution)/shard_map/ppermute | solution.py:8
  317.0 1.4 slice.419
  325.7 2.0 collective-permute-start.9
  334.1 37.1 %collective-permute-start.10 = (f32[278528]{0:T(1024)}, f32[278528]{0:T(1024)S(1)}, u32[]{:S(2)}, u32[]{:S(2)}) collective-permute-start(f32[278528]{0:T(1024)} %pad_maximum_fusion.5), channel_id=1, source_target_pairs={{0,64},{2,66},{4,68},{6,70},{8,72},{10,74},{12,76},{14,78},{16,80}... | collective-permute-start | bytes 3342344 | tf_op jit(solution)/shard_map/ppermute | solution.py:8
  371.3 58.9 %collective-permute-done.10 = f32[278528]{0:T(1024)S(1)} collective-permute-done((f32[278528]{0:T(1024)}, f32[278528]{0:T(1024)S(1)}, u32[]{:S(2)}, u32[]{:S(2)}) %collective-permute-start.10) | collective-permute-done | bytes 1114144 | tf_op jit(solution)/shard_map/ppermute | solution.py:8
  432.2 1.4 slice.429
  440.9 1.9 collective-permute-start.11
  449.3 2.7 collective-permute-start.12
  452.1 26.0 %collective-permute-done.12 = f32[278528]{0:T(1024)S(1)} collective-permute-done((f32[278528]{0:T(1024)}, f32[278528]{0:T(1024)S(1)}, u32[]{:S(2)}, u32[]{:S(2)}) %collective-permute-start.12) | collective-permute-done | bytes 1114144 | tf_op jit(solution)/shard_map/ppermute | solution.py:8
  480.1 1.4 slice.443
  488.6 1.9 collective-permute-start.13
  493.9 4.3 collective-permute-start.14
  499.3 7.7 %collective-permute-done.14 = f32[81920]{0:T(1024)S(1)} collective-permute-done((f32[81920]{0:T(1024)S(1)}, f32[81920]{0:T(1024)S(1)}, u32[]{:S(2)}, u32[]{:S(2)}) %collective-permute-start.14) | collective-permute-done | bytes 327712 | tf_op jit(solution)/shard_map/ppermute | solution.py:8
  508.8 1.3 fusion.31
  525.4 1.7 convolution_subtract_fusion.7
  (585 shorter events, 121.1 us)
Async XLA Ops:
  3.5 28.4 %collective-permute-start = (f32[278528]{0:T(1024)}, f32[278528]{0:T(1024)S(1)}, u32[]{:S(2)}, u32[]{:S(2)}) collective-permute-start(f32[278528]{0:T(1024)} %pad_maximum_fusion), channel_id=1, source_target_pairs={{0,2},{2,0},{4,6},{6,4},{8,10},{10,8},{12,14},{14,12},{16,18},{18,... | collective-permute-start | bytes 3342344 | tf_op jit(solution)/shard_map/ppermute | solution.py:8
  38.5 3.9 copy-start.126
  38.9 3.4 collective-permute-start.1
  41.5 2.9 copy-start.143
  44.8 41.4 %copy-start.124 = (f32[32,256]{1,0:T(8,128)}, f32[32,256]{1,0:T(8,128)S(1)}, u32[]{:S(2)}) copy-start(f32[32,256]{1,0:T(8,128)S(1)} %get-tuple-element.58) | copy-start | bytes 98308
  46.7 30.2 %collective-permute-start.2 = (f32[278528]{0:T(1024)}, f32[278528]{0:T(1024)S(1)}, u32[]{:S(2)}, u32[]{:S(2)}) collective-permute-start(f32[278528]{0:T(1024)} %pad_maximum_fusion.1), channel_id=1, source_target_pairs={{0,4},{2,6},{4,0},{6,2},{8,12},{10,14},{12,8},{14,10},{16,20},{18,... | collective-permute-start | bytes 3342344 | tf_op jit(solution)/shard_map/ppermute | solution.py:8
  86.5 3.5 copy-start.128
  86.5 3.0 copy-start.125
  87.3 2.7 copy-start.145
  87.6 3.4 collective-permute-start.3
  96.1 28.9 %collective-permute-start.4 = (f32[278528]{0:T(1024)}, f32[278528]{0:T(1024)S(1)}, u32[]{:S(2)}, u32[]{:S(2)}) collective-permute-start(f32[278528]{0:T(1024)} %pad_maximum_fusion.2), channel_id=1, source_target_pairs={{0,8},{2,10},{4,12},{6,14},{8,0},{10,2},{12,4},{14,6},{16,24},{18,... | collective-permute-start | bytes 3342344 | tf_op jit(solution)/shard_map/ppermute | solution.py:8
  134.6 3.4 copy-start.130
  135.7 3.4 collective-permute-start.5
  144.2 54.1 %collective-permute-start.6 = (f32[278528]{0:T(1024)}, f32[278528]{0:T(1024)S(1)}, u32[]{:S(2)}, u32[]{:S(2)}) collective-permute-start(f32[278528]{0:T(1024)} %pad_maximum_fusion.3), channel_id=1, source_target_pairs={{0,16},{2,18},{4,20},{6,22},{8,24},{10,26},{12,28},{14,30},{16,0},... | collective-permute-start | bytes 3342344 | tf_op jit(solution)/shard_map/ppermute | solution.py:8
  207.9 3.0 copy-start.132
  209.1 3.4 collective-permute-start.7
  217.5 97.4 %collective-permute-start.8 = (f32[278528]{0:T(1024)}, f32[278528]{0:T(1024)S(1)}, u32[]{:S(2)}, u32[]{:S(2)}) collective-permute-start(f32[278528]{0:T(1024)} %pad_maximum_fusion.4), channel_id=1, source_target_pairs={{0,32},{2,34},{4,36},{6,38},{8,40},{10,42},{12,44},{14,46},{16,48}... | collective-permute-start | bytes 3342344 | tf_op jit(solution)/shard_map/ppermute | solution.py:8
  324.6 3.1 copy-start.134
  325.3 2.8 copy-start.151
  325.7 3.4 collective-permute-start.9
  334.1 96.1 %collective-permute-start.10 = (f32[278528]{0:T(1024)}, f32[278528]{0:T(1024)S(1)}, u32[]{:S(2)}, u32[]{:S(2)}) collective-permute-start(f32[278528]{0:T(1024)} %pad_maximum_fusion.5), channel_id=1, source_target_pairs={{0,64},{2,66},{4,68},{6,70},{8,72},{10,74},{12,76},{14,78},{16,80}... | collective-permute-start | bytes 3342344 | tf_op jit(solution)/shard_map/ppermute | solution.py:8
  439.8 3.1 copy-start.136
  440.6 2.7 copy-start.153
  440.9 3.4 collective-permute-start.11
  449.3 28.7 %collective-permute-start.12 = (f32[278528]{0:T(1024)}, f32[278528]{0:T(1024)S(1)}, u32[]{:S(2)}, u32[]{:S(2)}) collective-permute-start(f32[278528]{0:T(1024)} %pad_maximum_fusion.6), channel_id=1, source_target_pairs={{0,128},{2,130},{4,132},{6,134},{8,136},{10,138},{12,140},{14,142}... | collective-permute-start | bytes 3342344 | tf_op jit(solution)/shard_map/ppermute | solution.py:8
  487.8 3.1 copy-start.155
  488.2 3.9 copy-start.39
  488.6 3.9 copy-start.28
  488.6 3.4 collective-permute-start.13
  492.1 6.2 %copy-start.30 = (f32[256,256]{1,0:T(8,128)}, f32[256,256]{1,0:T(8,128)S(1)}, u32[]{:S(2)}) copy-start(f32[256,256]{1,0:T(8,128)S(1)} %broadcast_select_fusion.2) | copy-start | bytes 786436
  493.6 5.7 %copy-start.32 = (f32[256,256]{1,0:T(8,128)}, f32[256,256]{1,0:T(8,128)S(1)}, u32[]{:S(2)}) copy-start(f32[256,256]{1,0:T(8,128)S(1)} %select_add_fusion) | copy-start | bytes 786436
  493.9 13.2 %collective-permute-start.14 = (f32[81920]{0:T(1024)S(1)}, f32[81920]{0:T(1024)S(1)}, u32[]{:S(2)}, u32[]{:S(2)}) collective-permute-start(f32[81920]{0:T(1024)S(1)} %pad_maximum_fusion.7), channel_id=1, source_target_pairs={{0,256},{2,258},{4,260},{6,262},{8,264},{10,266},{12,268},{14,270}... | collective-permute-start | bytes 983048 | tf_op jit(solution)/shard_map/ppermute | solution.py:8
  (147 other events, 215.6 us)
where the time goes:
time: 535 us; the launch traced here: 528 us
  waiting for transfers between devices  317 us (59%)
  starting transfers between devices  76.2 us (14%)
  matrix products  69.7 us (13%)
  local copies, waits for them, and re-layouts  44.7 us (8%)
  other arithmetic  15.6 us (3%)
    ppermute x15, waiting for transfers between devices, swapped(): lax.ppermute(shard, axis, [(i, i ^ 1 << bit) for i in range(lax.axis_size...  317 us
    ppermute x15, starting transfers between devices, swapped(): lax.ppermute(shard, axis, [(i, i ^ 1 << bit) for i in range(lax.axis_size...  76.2 us
    dot_general x110, matrix products, product(): jnp.dot(left, right, precision=lax.Precision.HIGHEST, preferred_element_t...  44.3 us
    dot_general x68, matrix products, against(): lax.dot_general(rows_in, matrix, (((1,), (1,)), ((), ())), precision=lax....  25.4 us
    unnamed x330, local copies, waits for them, and re-layouts  22 us
    slice x16, local copies, waits for them, and re-layouts, local(): spikes_in = arrived[:spikes_out.size].reshape(spikes_out.shape)  15.3 us
  transfers between devices with their start and end apart: 15, of which 15 were waited for; matrix products, arithmetic and copies ran while one was open for 1% of the time, Pallas kernels for 0%

commit v1 on v0

v1 whole, which is shorter than its diff:
```python
import functools
import jax
import jax.numpy as jnp
from jax import lax
from jax.experimental import pallas as pl
from jax.experimental.pallas import tpu as pltpu
from jax.sharding import PartitionSpec as P

MESH = pl.DeviceIdType.MESH


def split(x):
    high = x.astype(jnp.bfloat16)
    return high, (x - high.astype(jnp.float32)).astype(jnp.bfloat16)


def mm(left, right):
    left_high, left_low = left
    right_high, right_low = right
    dot = functools.partial(jnp.dot, preferred_element_type=jnp.float32)
    return dot(left_high, right_high) + (dot(left_high, right_low) + dot(left_low, right_high))


def kernel(
    levels, tips, sources, out,
    mate, cross, own, gs, goth, zrec, yrec, ysrc, trec, ebuf, esrc,
    msend, mrecv, csend, crecv, fsend, frecv, osend, orecv, gsend, grecv,
    zsend, zrecv, ysend, yrecv, vsend, vrecv, esend, erecv,
):
    s = lax.axis_index("slab")
    c = lax.axis_index("rhs")
    o = 1 - c
    block = tips.shape[1]
    half_size = block // 2
    half = pl.ds(pl.multiple_of(c * half_size, half_size), half_size)
    top = levels - 1

    def roles(d):
        p = lax.div(d, 3)
        q = lax.div(2 * d, 3)
        off = lax.rem(s, d)
        h = lax.rem(lax.div(s, d), 2)
        act_off = q + h * (p - q)
        ret_off = p + h * (q - p)
        base = s - off
        active = off == act_off
        retiring = jnp.logical_and(off == ret_off, p != q)
        partner = base + (1 - 2 * h) * d + ret_off
        return active, retiring, partner, base + act_off, base + ret_off

    def remote(src, dst, send, recv, slab, core):
        return pltpu.make_async_remote_copy(
            src_ref=src, dst_ref=dst, send_sem=send, recv_sem=recv,
            device_id=(slab, core), device_id_type=MESH,
        )

    def mate_copy(k, j):
        ref = mate.at[k, j, half]
        return remote(ref, ref, msend.at[k, j], mrecv.at[k, j], s, o)

    def cross_copy(k, j, partner):
        return remote(
            mate.at[k, j, half], cross.at[k, j, half], csend.at[k, j], crecv.at[k, j], partner, c
        )

    def cross_forward(k, j):
        ref = cross.at[k, j, half]
        return remote(ref, ref, fsend.at[k, j], frecv.at[k, j], s, o)

    def own_copy(k, j, target):
        return remote(
            mate.at[k, j, half], own.at[k, j], osend.at[k, j], orecv.at[k, j], target, c
        )

    def source_copy(k, j, partner):
        return remote(gs.at[k, j], goth.at[k, j], gsend.at[k, j], grecv.at[k, j], partner, c)

    def z_copy(k):
        ref = zrec.at[k, half]
        return remote(ref, ref, zsend.at[k], zrecv.at[k], s, o)

    def y_copy(k, partner):
        return remote(ysrc.at[k], yrec.at[k, half], ysend.at[k], yrecv.at[k], partner, c)

    def y_forward(k):
        ref = yrec.at[k, half]
        return remote(ref, ref, vsend.at[k], vrecv.at[k], s, o)

    def edge_copy(k, target):
        return remote(esrc.at[k], ebuf.at[k - 1], esend.at[k], erecv.at[k], target, c)

    barrier = pltpu.get_barrier_semaphore()

    def greet(slab, core):
        pl.semaphore_signal(barrier, inc=1, device_id=(slab, core), device_id_type=MESH)

    greet(s, o)
    greeted = 1
    for k in range(levels):
        active, retiring, partner, target, retiree = roles(2**k)

        @pl.when(active)
        def _():
            greet(partner, c)
            if k > 0:
                greet(retiree, c)

        greeted = greeted + jnp.where(active, 2 if k > 0 else 1, 0)
        if k > 0:

            @pl.when(retiring)
            def _():
                greet(target, c)

            greeted = greeted + jnp.where(retiring, 1, 0)

    h0 = lax.rem(s, 2)
    for j in range(2):
        mate[0, j] = tips[2 * (1 - h0) + j]
        own[0, j] = tips[2 * h0 + j, half]
    gs[0, 0] = sources[1 - h0]
    gs[0, 1] = sources[h0]
    pl.semaphore_wait(barrier, greeted)

    first_partner = roles(1)[2]
    cross_copy(0, 0, first_partner).start()
    source_copy(0, 0, first_partner).start()
    cross_copy(0, 1, first_partner).start()
    source_copy(0, 1, first_partner).start()

    def solved(rows, coupling):
        power = split(coupling)
        rows = rows + mm(split(rows), power)
        for _ in range(3):
            power = split(mm(power, power))
            rows = rows + mm(split(rows), power)
        return rows

    def up(k, d):
        active, _, partner, _, retiree = roles(d)
        next_active, next_retiring, next_partner, next_target, _ = roles(2 * d)
        below_top = k + 1 < top

        @pl.when(active)
        def _():
            cross_copy(k, 0, partner).wait_recv()
            cross_forward(k, 0).start()
            source_copy(k, 0, partner).wait_recv()

            @pl.when(k > 0)
            def _():
                mate_copy(k, 0).wait_recv()
                own_copy(k, 1, retiree).wait_recv()

            mate_near = split(mate[k, 0])
            rhs = gs[k, 0] - mm(split(goth[k, 0]), mate_near)
            cross_forward(k, 0).wait_recv()
            cross_near = split(cross[k, 0])
            coupling = mm(cross_near, mate_near)
            rows = jnp.concatenate([own[k, 1], rhs], axis=0)
            y = solved(rows, coupling)
            y_parts = split(y)
            z = mm(y_parts, cross_near)
            z_own = z[:half_size]
            t = goth[k, 0] - z[half_size:]
            trec[k] = t
            ysrc[k] = y[:half_size]
            zrec[k, half] = z_own

            cross_copy(k, 1, partner).wait_recv()
            cross_forward(k, 1).start()
            cross_copy(k, 0, partner).wait_send()
            cross_copy(k, 1, partner).wait_send()

            @pl.when(k > 0)
            def _():
                y_copy(k - 1, roles(lax.div(d, 2))[2]).start()
                mate_copy(k, 1).wait_recv()
                own_copy(k, 0, retiree).wait_recv()

            near = jnp.concatenate([own[k, 0], gs[k, 1]], axis=0) + mm(
                split(jnp.concatenate([z_own, -t], axis=0)), split(mate[k, 1])
            )
            mate[k + 1, 0, half] = near[:half_size]
            gs[k + 1, 0] = near[half_size:]

            @pl.when(next_active)
            def _():
                cross_copy(k + 1, 0, next_partner).start()
                mate_copy(k + 1, 0).start()
                source_copy(k + 1, 0, next_partner).start()

            @pl.when(jnp.logical_and(next_retiring, below_top))
            def _():
                own_copy(k + 1, 0, next_target).start()

            source_copy(k, 1, partner).wait_recv()
            cross_forward(k, 1).wait_recv()
            product = mm(y_parts, split(cross[k, 1]))
            mate[k + 1, 1, half] = -product[:half_size]
            gs[k + 1, 1] = goth[k, 1] - product[half_size:]

            @pl.when(jnp.logical_and(next_active, below_top))
            def _():
                cross_copy(k + 1, 1, next_partner).start()
                mate_copy(k + 1, 1).start()
                source_copy(k + 1, 1, next_partner).start()

            @pl.when(jnp.logical_and(next_retiring, below_top))
            def _():
                own_copy(k + 1, 1, next_target).start()

            z_copy(k).start()

            @pl.when(jnp.logical_and(next_retiring, below_top))
            def _():
                own_copy(k + 1, 0, next_target).wait_send()
                own_copy(k + 1, 1, next_target).wait_send()

            @pl.when(next_retiring)
            def _():
                y_copy(k, partner).start()

        return 2 * d

    lax.fori_loop(0, top, up, jnp.int32(1))

    def forward_y(k, d):
        active, _, partner, _, _ = roles(d)

        @pl.when(active)
        def _():
            y_copy(k, partner).wait_recv()
            y_forward(k).start()

        return 2 * d

    lax.fori_loop(0, top - 1, forward_y, jnp.int32(1))

    top_active, _, top_partner, _, top_retiree = roles(2**top)

    @pl.when(top_active)
    def _():
        cross_copy(top, 0, top_partner).wait_recv()
        cross_forward(top, 0).start()
        source_copy(top, 0, top_partner).wait_recv()
        cross_copy(top, 0, top_partner).wait_send()
        y_copy(top - 1, roles(2 ** (top - 1))[2]).start()
        mate_copy(top, 0).wait_recv()
        mate_near = split(mate[top, 0])
        rhs = gs[top, 0] - mm(split(goth[top, 0]), mate_near)
        cross_forward(top, 0).wait_recv()
        cross_near = split(cross[top, 0])
        coupling = mm(cross_near, mate_near)
        solution_rows = solved(rhs, coupling)
        t = goth[top, 0] - mm(split(solution_rows), cross_near)
        esrc[top, 0] = jnp.zeros_like(t)
        esrc[top, 1] = t
        edge_copy(top, top_retiree).start()
        ebuf[top - 1, 0] = t
        ebuf[top - 1, 1] = jnp.zeros_like(t)

    forward_y(top - 1, 2 ** (top - 1))

    def down(index, d):
        k = top - 1 - index
        active, _, _, _, retiree = roles(d)
        _, was_retiring, _, _, _ = roles(2 * d)

        @pl.when(active)
        def _():
            z_copy(k).wait_recv()
            y_forward(k).wait_recv()
            z_parts = split(zrec[k])
            y_parts = split(yrec[k])

            @pl.when(was_retiring)
            def _():
                edge_copy(k + 1, s).wait_recv()

            own_edge = ebuf[k, 0]
            other_edge = ebuf[k, 1]
            new = trec[k] + mm(split(own_edge), z_parts) - mm(split(other_edge), y_parts)

            @pl.when(k > 0)
            def _():
                esrc[k, 0] = own_edge
                esrc[k, 1] = new
                edge_copy(k, retiree).start()
                ebuf[k - 1, 0] = new
                ebuf[k - 1, 1] = own_edge

            @pl.when(k == 0)
            def _():
                out[h0] = own_edge
                out[1 - h0] = new

        return lax.div(d, 2)

    lax.fori_loop(0, top, down, jnp.int32(2 ** (top - 1)))

    def finish(k, d):
        active, _, partner, _, retiree = roles(d)

        @pl.when(active)
        def _():
            source_copy(k, 0, partner).wait_send()
            cross_forward(k, 0).wait_send()

            @pl.when(k > 0)
            def _():
                mate_copy(k, 0).wait_send()
                edge_copy(k, retiree).wait_send()

            @pl.when(k < top)
            def _():
                source_copy(k, 1, partner).wait_send()
                cross_forward(k, 1).wait_send()
                z_copy(k).wait_send()
                y_copy(k, partner).wait_send()
                y_forward(k).wait_send()

            @pl.when(jnp.logical_and(k > 0, k < top))
            def _():
                mate_copy(k, 1).wait_send()

        return 2 * d

    lax.fori_loop(0, levels, finish, jnp.int32(1))


def local(right_spike, left_spike, local_rhs):
    block = right_spike.shape[1]
    part_rows = right_spike.shape[0]
    columns = local_rhs.shape[0]
    levels = lax.axis_size("slab").bit_length() - 1
    last = part_rows - block
    tips = jnp.stack(
        [left_spike[:block].T, left_spike[last:].T, right_spike[last:].T, right_spike[:block].T]
    )
    sources = jnp.stack([local_rhs[:, :block], local_rhs[:, last:]])
    half = block // 2
    f32 = jnp.float32
    pair = pltpu.SemaphoreType.DMA((levels, 2))
    one = pltpu.SemaphoreType.DMA((levels,))
    vmem = pl.BlockSpec(memory_space=pltpu.VMEM)
    edges = pl.pallas_call(
        functools.partial(kernel, levels),
        out_shape=jax.ShapeDtypeStruct((2, columns, block), f32),
        in_specs=[vmem, vmem],
        out_specs=vmem,
        scratch_shapes=[
            pltpu.VMEM((levels, 2, block, block), f32),
            pltpu.VMEM((levels, 2, block, block), f32),
            pltpu.VMEM((levels, 2, half, block), f32),
            pltpu.VMEM((levels, 2, columns, block), f32),
            pltpu.VMEM((levels, 2, columns, block), f32),
            pltpu.VMEM((levels, block, block), f32),
            pltpu.VMEM((levels, block, block), f32),
            pltpu.VMEM((levels, half, block), f32),
            pltpu.VMEM((levels, columns, block), f32),
            pltpu.VMEM((levels, 2, columns, block), f32),
            pltpu.VMEM((levels, 2, columns, block), f32),
        ]
        + [pair] * 10
        + [one] * 8,
        compiler_params=pltpu.CompilerParams(
            collective_id=0, has_side_effects=True, vmem_limit_bytes=40 * 2**20
        ),
    )(tips, sources)

    def against(rows, matrix):
        return lax.dot_general(
            rows,
            matrix,
            (((1,), (1,)), ((), ())),
            precision=lax.Precision.HIGH,
            preferred_element_type=f32,
        )

    return local_rhs - against(edges[1], right_spike) - against(edges[0], left_spike)


def solution(mesh):
    return jax.shard_map(
        local,
        mesh=mesh,
        in_specs=(P("slab", None), P("slab", None), P("rhs", "slab")),
        out_specs=P("rhs", "slab"),
        check_vma=False,
    )
```

time: 535 us -> 169 us (0.32)
  the two profiles are of different devices: /device:TPU:138 before, /device:TPU:8 now
where the time goes in v1:
time: 169 us
  Pallas kernels  164 us (97%)
  local copies, waits for them, and re-layouts  2.53 us (1%)
  matrix products  1.8 us (1%)
    pallas_call x1, Pallas kernels, local(): pl.pallas_call(functools.partial(kernel, levels), out_shape=jax.ShapeDtyp...  164 us

profile of v1, /device:TPU:8, one launch (start us, length us, event | category | flops | bytes accessed | tf_op | source)
XLA Modules:
  0.0 168.6 jit_solution(15264862630969040110)
XLA Ops:
  0.0 0.0 copy-start
  0.0 1.2 fusion.4
  1.2 0.1 copy.8
  1.3 0.1 copy.9
  1.4 0.0 copy-done
  1.5 0.1 copy.10
  1.6 0.1 copy.11
  1.8 0.0 copy-start.2
  1.8 0.1 pad_maximum_fusion.tips
  1.9 0.8 copy-done.2
  2.7 0.0 copy-start.1
  2.7 164.1 %shard_map.37 = f32[2,32,256]{2,1,0:T(8,128)S(1)} custom-call(f32[4,256,256]{2,1,0:T(8,128)S(1)} %pad_maximum_fusion.tips, f32[2,32,256]{2,1,0:T(8,128)S(1)} %pad_maximum_fusion.1.sources), custom_call_target="tpu_custom_call" | custom-call | tf_op jit(solution)/shard_map/pallas_call | solution.py:347
  166.8 0.6 convolution_subtract_fusion.1
  167.4 0.0 copy-done.1
  167.4 1.2 convolution_subtract_fusion
  (3 shorter events, 0.0 us)
Async XLA Ops:
  0.0 1.4 copy-start
  1.8 0.9 copy-start.2
  2.7 164.7 %copy-start.1 = (f32[1024,256]{1,0:T(8,128)S(1)}, f32[1024,256]{1,0:T(8,128)}, u32[]{:S(2)}) copy-start(f32[1024,256]{1,0:T(8,128)} %param.4) | copy-start | bytes 3145732

commit v2 on v1

v2 whole, which is shorter than its diff:
```python
import functools
import jax
import jax.numpy as jnp
from jax import lax
from jax.experimental import pallas as pl
from jax.experimental.pallas import tpu as pltpu
from jax.sharding import PartitionSpec as P

MESH = pl.DeviceIdType.MESH


def split(x):
    high = x.astype(jnp.bfloat16)
    return high, (x - high.astype(jnp.float32)).astype(jnp.bfloat16)


def mm(left, right):
    left_high, left_low = left
    right_high, right_low = right
    return jnp.dot(
        jnp.concatenate([left_high, left_high, left_low], axis=1),
        jnp.concatenate([right_high, right_low, right_high], axis=0),
        preferred_element_type=jnp.float32,
    )


def places(levels, left_level, outer_level):
    p = q = 0
    rows = []
    for k in range(levels):
        d = 2**k
        if k == left_level and k < levels - 1:
            rows.append((d, p, p, q, q, 0, 1))
            p, q = p, d + p
        elif k == outer_level and k < levels - 1:
            rows.append((d, p, q, q, p, 0, 0))
            p, q = p, d + q
        else:
            rows.append((d, q, p, p, q, 1, 1))
            p, q = q, d + p
    return rows


LEFT_LEVEL = 2
OUTER_LEVEL = 6


def kernel(
    levels, tips, sources, out,
    side, mate, cross, own, gs, goth, zrec, yrec, ysrc, trec, ebuf, esrc, rec_high, rec_low,
    msend, mrecv, tsend, trecv, csend, crecv, fsend, frecv, osend, orecv, gsend, grecv,
    esend, erecv, kept_sem, zsend, zrecv, ysend, yrecv, vsend, vrecv,
):
    s = lax.axis_index("slab")
    c = lax.axis_index("rhs")
    o = 1 - c
    block = tips.shape[1]
    half_size = block // 2
    half = pl.ds(pl.multiple_of(c * half_size, half_size), half_size)
    other_half = pl.ds(pl.multiple_of(o * half_size, half_size), half_size)
    top = levels - 1
    rows_of = places(levels, LEFT_LEVEL, OUTER_LEVEL)

    def table(k, column):
        values = [row[column] for row in rows_of]
        if isinstance(k, int):
            return values[k]
        value = jnp.int32(values[0])
        for i in range(1, levels):
            value = jnp.where(k == i, values[i], value)
        return value

    def roles(k):
        d, act0, act1, ret0, ret1, keep0, keep1 = [table(k, i) for i in range(7)]
        off = lax.rem(s, d)
        h = lax.rem(lax.div(s, d), 2)
        act_off = act0 + h * (act1 - act0)
        ret_off = ret0 + h * (ret1 - ret0)
        keep = keep0 + h * (keep1 - keep0)
        base = s - off
        other = base + (1 - 2 * h) * d
        return {
            "active": off == act_off,
            "retiring": jnp.logical_and(off == ret_off, act_off != ret_off),
            "keep": keep,
            "keeps": keep == 1,
            "target": base + act_off,
            "retiree": base + ret_off,
            "partner": other + act1 + h * (act0 - act1),
            "other_retiree": other + ret1 + h * (ret0 - ret1),
        }

    def both(*conditions):
        return functools.reduce(jnp.logical_and, conditions)

    def remote(src, dst, send, recv, slab, core):
        return pltpu.make_async_remote_copy(
            src_ref=src, dst_ref=dst, send_sem=send, recv_sem=recv,
            device_id=(slab, core), device_id_type=MESH,
        )

    def mate_copy(k, j, rows=half):
        ref = mate.at[k, j, rows]
        return remote(ref, ref, msend.at[k, j], mrecv.at[k, j], s, o)

    def mate_send(k, j, target):
        return remote(
            side.at[k, j], mate.at[k, j, half], tsend.at[k, j], trecv.at[k, j], target, c
        )

    def cross_copy(k, j, partner):
        return remote(
            side.at[k, j], cross.at[k, j, half], csend.at[k, j], crecv.at[k, j], partner, c
        )

    def cross_forward(k, j, rows=half):
        ref = cross.at[k, j, rows]
        return remote(ref, ref, fsend.at[k, j], frecv.at[k, j], s, o)

    def own_copy(k, j, target):
        return remote(side.at[k, j], own.at[k, j], osend.at[k, j], orecv.at[k, j], target, c)

    def own_keep(k, j):
        return pltpu.make_async_copy(side.at[k, j], own.at[k, j], kept_sem.at[k, j])

    def source_copy(k, j, partner):
        return remote(gs.at[k, j], goth.at[k, j], gsend.at[k, j], grecv.at[k, j], partner, c)

    def z_copy(k, rows=half):
        ref = zrec.at[k, rows]
        return remote(ref, ref, zsend.at[k], zrecv.at[k], s, o)

    def y_copy(k, partner):
        return remote(ysrc.at[k], yrec.at[k, half], ysend.at[k], yrecv.at[k], partner, c)

    def y_forward(k, rows=half):
        ref = yrec.at[k, rows]
        return remote(ref, ref, vsend.at[k], vrecv.at[k], s, o)

    def old_edge_copy(k, keep, target):
        return remote(
            ebuf.at[k, 0], ebuf.at[k - 1, 1 - keep], esend.at[k, 0], erecv.at[k, 0], target, c
        )

    def new_edge_copy(k, keep, target):
        return remote(
            esrc.at[k], ebuf.at[k - 1, keep], esend.at[k, 1], erecv.at[k, 1], target, c
        )

    barrier = pltpu.get_barrier_semaphore()

    def greet(slab, core):
        pl.semaphore_signal(barrier, inc=1, device_id=(slab, core), device_id_type=MESH)

    greet(s, o)
    greet(roles(0)["partner"], c)
    greeted = 2
    for k in range(1, levels):
        r = roles(k)

        @pl.when(r["active"])
        def _():
            greet(r["retiree"], c)

        @pl.when(r["retiring"])
        def _():
            greet(r["target"], c)

        takes_part = jnp.logical_or(r["active"], r["retiring"])

        @pl.when(takes_part)
        def _():
            greet(r["partner"], c)
            greet(r["other_retiree"], c)

        greeted = greeted + jnp.where(takes_part, 3, 0)

    h0 = lax.rem(s, 2)
    for j in range(2):
        mate[0, j] = tips[2 * (1 - h0) + j]
        side[0, j] = tips[2 * (1 - h0) + j, half]
        own[0, j] = tips[2 * h0 + j, half]
    gs[0, 0] = sources[1 - h0]
    gs[0, 1] = sources[h0]
    pl.semaphore_wait(barrier, greeted)

    first_partner = roles(0)["partner"]
    for j in range(2):
        cross_copy(0, j, first_partner).start()
        source_copy(0, j, first_partner).start()

    def solved(rows, coupling):
        power = split(coupling)
        rows = rows + mm(split(rows), power)
        for _ in range(2):
            power = split(mm(power, power))
            rows = rows + mm(split(rows), power)
        dot = functools.partial(jnp.dot, preferred_element_type=jnp.float32)
        last = dot(power[0], power[0]).astype(jnp.bfloat16)
        return rows + dot(rows.astype(jnp.bfloat16), last)

    def send_side(k, j, r, value):
        below_top = k < top
        retiring = r["retiring"] if j == 0 else both(r["retiring"], below_top)
        active = r["active"] if j == 0 else both(r["active"], below_top)
        keeps = r["keeps"]

        @pl.when(both(active, keeps))
        def _():
            cross_copy(k, j, r["partner"]).start()
            mate[k, j, half] = value
            mate_copy(k, j).start()
            source_copy(k, j, r["partner"]).start()

        @pl.when(both(active, jnp.logical_not(keeps)))
        def _():
            own_keep(k, j).start()

        @pl.when(both(retiring, keeps, below_top))
        def _():
            own_copy(k, j, r["target"]).start()

        @pl.when(both(retiring, jnp.logical_not(keeps)))
        def _():
            mate_send(k, j, r["target"]).start()
            cross_copy(k, j, r["partner"]).start()
            source_copy(k, j, r["partner"]).start()

    def up(k, carry):
        r = roles(k)
        following = roles(k + 1)
        keep = r["keep"]
        partner = r["partner"]
        retiree = r["retiree"]
        moved = both(k > 0, jnp.logical_not(r["keeps"]))
        kept = both(k > 0, r["keeps"])

        @pl.when(r["active"])
        def _():
            @pl.when(moved)
            def _():
                mate_send(k, 0, r["target"]).wait_recv()
                mate_copy(k, 0).start()

            cross_copy(k, 0, partner).wait_recv()
            cross_forward(k, 0).start()
            source_copy(k, 0, partner).wait_recv()

            @pl.when(k > 0)
            def _():
                mate_copy(k, 0, other_half).wait_recv()

            @pl.when(kept)
            def _():
                own_copy(k, 1, retiree).wait_recv()

            @pl.when(moved)
            def _():
                own_keep(k, 1).wait()

            mate_near = split(mate[k, 0])
            rhs = gs[k, 1 - keep] - mm(split(goth[k, 0]), mate_near)
            cross_forward(k, 0, other_half).wait_recv()
            cross_near = split(cross[k, 0])
            coupling = mm(cross_near, mate_near)
            y = solved(jnp.concatenate([own[k, 1], rhs], axis=0), coupling)
            y_parts = split(y)
            z = mm(y_parts, cross_near)
            z_own = z[:half_size]
            t = goth[k, 0] - z[half_size:]
            trec[k] = t
            ysrc[k] = y[:half_size]
            zrec[k, half] = z_own

            @pl.when(moved)
            def _():
                mate_send(k, 1, r["target"]).wait_recv()
                mate_copy(k, 1).start()

            @pl.when(k > 0)
            def _():
                mate_copy(k, 1, other_half).wait_recv()

            @pl.when(kept)
            def _():
                own_copy(k, 0, retiree).wait_recv()

            @pl.when(moved)
            def _():
                own_keep(k, 0).wait()

            near = jnp.concatenate([own[k, 0], gs[k, keep]], axis=0) + mm(
                split(jnp.concatenate([z_own, -t], axis=0)), split(mate[k, 1])
            )
            side[k + 1, 0] = near[:half_size]
            gs[k + 1, 0] = near[half_size:]
            send_side(k + 1, 0, following, near[:half_size])

            cross_copy(k, 1, partner).wait_recv()
            cross_forward(k, 1).start()
            source_copy(k, 1, partner).wait_recv()
            cross_forward(k, 1, other_half).wait_recv()
            product = mm(y_parts, split(cross[k, 1]))
            side[k + 1, 1] = -product[:half_size]
            gs[k + 1, 1] = goth[k, 1] - product[half_size:]
            send_side(k + 1, 1, following, -product[:half_size])
            z_copy(k).start()

            @pl.when(both(following["retiring"], k + 1 < top))
            def _():
                @pl.when(following["keeps"])
                def _():
                    for j in range(2):
                        own_copy(k + 1, j, following["target"]).wait_send()

                @pl.when(jnp.logical_not(following["keeps"]))
                def _():
                    for j in range(2):
                        mate_send(k + 1, j, following["target"]).wait_send()
                        cross_copy(k + 1, j, following["partner"]).wait_send()

            y_copy(k, partner).start()

        return carry

    lax.fori_loop(0, top, up, 0)

    def forward_y(k, carry):
        r = roles(k)

        @pl.when(r["active"])
        def _():
            y_copy(k, r["partner"]).wait_recv()
            y_forward(k).start()

        return carry

    lax.fori_loop(0, top - 1, forward_y, 0)

    r_top = roles(top)

    @pl.when(r_top["active"])
    def _():
        cross_copy(top, 0, r_top["partner"]).wait_recv()
        cross_forward(top, 0).start()
        source_copy(top, 0, r_top["partner"]).wait_recv()
        mate_copy(top, 0, other_half).wait_recv()
        mate_near = split(mate[top, 0])
        rhs = gs[top, 0] - mm(split(goth[top, 0]), mate_near)
        cross_forward(top, 0, other_half).wait_recv()
        cross_near = split(cross[top, 0])
        coupling = mm(cross_near, mate_near)
        t = goth[top, 0] - mm(split(solved(rhs, coupling)), cross_near)
        ebuf[top, 0] = jnp.zeros_like(t)
        esrc[top] = t
        new_edge_copy(top, 1, r_top["retiree"]).start()
        old_edge_copy(top, 1, r_top["retiree"]).start()
        ebuf[top - 1, 0] = t
        ebuf[top - 1, 1] = jnp.zeros_like(t)

    forward_y(top - 1, 0)

    def down(index, carry):
        k = top - 1 - index
        r = roles(k)
        above = roles(k + 1)
        keep = r["keep"]

        @pl.when(r["active"])
        def _():
            z_copy(k, other_half).wait_recv()
            y_forward(k, other_half).wait_recv()
            for part, rec in enumerate((zrec, yrec)):
                high, low = split(rec[k])
                rec_high[part * block : (part + 1) * block] = high
                rec_low[part * block : (part + 1) * block] = low

            @pl.when(above["retiring"])
            def _():
                old_edge_copy(k + 1, above["keep"], s).wait_recv()
                new_edge_copy(k + 1, above["keep"], s).wait_recv()

            @pl.when(k > 0)
            def _():
                old_edge_copy(k, keep, r["retiree"]).start()

            own_edge = ebuf[k, 0]
            high, low = split(jnp.concatenate([own_edge, -ebuf[k, 1]], axis=1))
            dot = functools.partial(jnp.dot, preferred_element_type=jnp.float32)
            columns = own_edge.shape[0]
            stacked = dot(jnp.concatenate([high, low], axis=0), rec_high[...])
            new = trec[k] + (
                stacked[:columns] + (stacked[columns:] + dot(high, rec_low[...]))
            )

            @pl.when(k > 0)
            def _():
                esrc[k] = new
                new_edge_copy(k, keep, r["retiree"]).start()
                ebuf[k - 1, 1 - keep] = new
                ebuf[k - 1, keep] = own_edge

            @pl.when(k == 0)
            def _():
                out[h0] = own_edge
                out[1 - h0] = new

        return carry

    lax.fori_loop(0, top, down, 0)

    def finish(k, carry):
        r = roles(k)
        keeps = r["keeps"]
        below_top = k < top
        sends_cross = jnp.logical_or(
            both(r["active"], keeps), both(r["retiring"], jnp.logical_not(keeps))
        )

        @pl.when(sends_cross)
        def _():
            source_copy(k, 0, r["partner"]).wait_send()

            @pl.when(below_top)
            def _():
                source_copy(k, 1, r["partner"]).wait_send()

        @pl.when(both(r["active"], keeps))
        def _():
            cross_copy(k, 0, r["partner"]).wait_send()

            @pl.when(below_top)
            def _():
                cross_copy(k, 1, r["partner"]).wait_send()

        @pl.when(r["active"])
        def _():
            cross_forward(k, 0).wait_send()

            @pl.when(k > 0)
            def _():
                mate_copy(k, 0).wait_send()
                old_edge_copy(k, r["keep"], r["retiree"]).wait_send()
                new_edge_copy(k, r["keep"], r["retiree"]).wait_send()

            @pl.when(below_top)
            def _():
                cross_forward(k, 1).wait_send()
                z_copy(k).wait_send()
                y_copy(k, r["partner"]).wait_send()
                y_forward(k).wait_send()

            @pl.when(both(k > 0, below_top))
            def _():
                mate_copy(k, 1).wait_send()

        return carry

    lax.fori_loop(0, levels, finish, 0)


def local(right_spike, left_spike, local_rhs):
    block = right_spike.shape[1]
    part_rows = right_spike.shape[0]
    columns = local_rhs.shape[0]
    levels = lax.axis_size("slab").bit_length() - 1
    last = part_rows - block
    tips = jnp.stack(
        [left_spike[:block].T, left_spike[last:].T, right_spike[last:].T, right_spike[:block].T]
    )
    sources = jnp.stack([local_rhs[:, :block], local_rhs[:, last:]])
    half = block // 2
    f32 = jnp.float32
    pair = pltpu.SemaphoreType.DMA((levels, 2))
    one = pltpu.SemaphoreType.DMA((levels,))
    vmem = pl.BlockSpec(memory_space=pltpu.VMEM)
    edges = pl.pallas_call(
        functools.partial(kernel, levels),
        out_shape=jax.ShapeDtypeStruct((2, columns, block), f32),
        in_specs=[vmem, vmem],
        out_specs=vmem,
        scratch_shapes=[
            pltpu.VMEM((levels, 2, half, block), f32),
            pltpu.VMEM((levels, 2, block, block), f32),
            pltpu.VMEM((levels, 2, block, block), f32),
            pltpu.VMEM((levels, 2, half, block), f32),
            pltpu.VMEM((levels, 2, columns, block), f32),
            pltpu.VMEM((levels, 2, columns, block), f32),
            pltpu.VMEM((levels, block, block), f32),
            pltpu.VMEM((levels, block, block), f32),
            pltpu.VMEM((levels, half, block), f32),
            pltpu.VMEM((levels, columns, block), f32),
            pltpu.VMEM((levels, 2, columns, block), f32),
            pltpu.VMEM((levels, columns, block), f32),
            pltpu.VMEM((2 * block, block), jnp.bfloat16),
            pltpu.VMEM((2 * block, block), jnp.bfloat16),
        ]
        + [pair] * 15
        + [one] * 6,
        compiler_params=pltpu.CompilerParams(
            collective_id=0, has_side_effects=True, vmem_limit_bytes=40 * 2**20
        ),
    )(tips, sources)

    def against(rows, matrix):
        return lax.dot_general(
            rows,
            matrix,
            (((1,), (1,)), ((), ())),
            precision=lax.Precision.HIGH,
            preferred_element_type=f32,
        )

    return local_rhs - against(edges[1], right_spike) - against(edges[0], left_spike)


def solution(mesh):
    return jax.shard_map(
        local,
        mesh=mesh,
        in_specs=(P("slab", None), P("slab", None), P("rhs", "slab")),
        out_specs=P("rhs", "slab"),
        check_vma=False,
    )
```

time: 169 us -> 134 us (0.79)
  the two profiles are of different devices: /device:TPU:8 before, /device:TPU:30 now
where the time goes in v2:
time: 134 us
  Pallas kernels  129 us (96%)
  local copies, waits for them, and re-layouts  2.53 us (2%)
  matrix products  1.8 us (1%)
    pallas_call x1, Pallas kernels, local(): pl.pallas_call(functools.partial(kernel, levels), out_shape=jax.ShapeDtyp...  129 us

profile of v2, /device:TPU:30, one launch (start us, length us, event | category | flops | bytes accessed | tf_op | source)
XLA Modules:
  0.0 133.7 jit_solution(18139548984961131154)
XLA Ops:
  0.0 0.0 copy-start
  0.0 1.2 fusion.4
  1.2 0.1 copy.8
  1.3 0.1 copy.9
  1.4 0.0 copy-done
  1.5 0.1 copy.10
  1.6 0.1 copy.11
  1.8 0.0 copy-start.2
  1.8 0.1 pad_maximum_fusion.tips
  1.9 0.8 copy-done.2
  2.7 0.0 copy-start.1
  2.7 129.1 %shard_map.37 = f32[2,32,256]{2,1,0:T(8,128)S(1)} custom-call(f32[4,256,256]{2,1,0:T(8,128)S(1)} %pad_maximum_fusion.tips, f32[2,32,256]{2,1,0:T(8,128)S(1)} %pad_maximum_fusion.1.sources), custom_call_target="tpu_custom_call" | custom-call | tf_op jit(solution)/shard_map/pallas_call | solution.py:477
  131.8 0.6 convolution_subtract_fusion.1
  132.4 0.0 copy-done.1
  132.4 1.2 convolution_subtract_fusion
  (3 shorter events, 0.0 us)
Async XLA Ops:
  0.0 1.4 %copy-start = (f32[1024,256]{1,0:T(8,128)S(1)}, f32[1024,256]{1,0:T(8,128)}, u32[]{:S(2)}) copy-start(f32[1024,256]{1,0:T(8,128)} %param.3) | copy-start | bytes 3145732
  1.8 0.9 copy-start.2
  2.7 129.7 %copy-start.1 = (f32[1024,256]{1,0:T(8,128)S(1)}, f32[1024,256]{1,0:T(8,128)}, u32[]{:S(2)}) copy-start(f32[1024,256]{1,0:T(8,128)} %param.4) | copy-start | bytes 3145732

commit v3 on v2

--- a/solution.py
+++ b/solution.py
@@ -48,6 +48,7 @@
 def kernel(
     levels, tips, sources, out,
     side, mate, cross, own, gs, goth, zrec, yrec, ysrc, trec, ebuf, esrc, rec_high, rec_low,
+    mate_high, mate_low,
     msend, mrecv, tsend, trecv, csend, crecv, fsend, frecv, osend, orecv, gsend, grecv,
     esend, erecv, kept_sem, zsend, zrecv, ysend, yrecv, vsend, vrecv,
 ):
@@ -189,15 +190,16 @@
         cross_copy(0, j, first_partner).start()
         source_copy(0, j, first_partner).start()
 
-    def solved(rows, coupling):
+    def inverse_rest(coupling):
         power = split(coupling)
-        rows = rows + mm(split(rows), power)
+        rest = coupling
         for _ in range(2):
-            power = split(mm(power, power))
-            rows = rows + mm(split(rows), power)
+            square = mm(power, power)
+            power = split(square)
+            rest = rest + square + mm(split(rest), power)
         dot = functools.partial(jnp.dot, preferred_element_type=jnp.float32)
-        last = dot(power[0], power[0]).astype(jnp.bfloat16)
-        return rows + dot(rows.astype(jnp.bfloat16), last)
+        last = dot(power[0], power[0])
+        return rest + last + dot(rest.astype(jnp.bfloat16), last.astype(jnp.bfloat16))
 
     def send_side(k, j, r, value):
         below_top = k < top
@@ -235,36 +237,52 @@
         moved = both(k > 0, jnp.logical_not(r["keeps"]))
         kept = both(k > 0, r["keeps"])
 
+        def split_mate(j):
+            mate_high[j], mate_low[j] = split(mate[k, j])
+
         @pl.when(r["active"])
         def _():
             @pl.when(moved)
             def _():
                 mate_send(k, 0, r["target"]).wait_recv()
                 mate_copy(k, 0).start()
+
+            @pl.when(k > 0)
+            def _():
+                mate_copy(k, 0, other_half).wait_recv()
+
+            split_mate(0)
+
+            @pl.when(kept)
+            def _():
+                mate_copy(k, 1, other_half).wait_recv()
+
+            @pl.when(jnp.logical_not(moved))
+            def _():
+                split_mate(1)
 
             cross_copy(k, 0, partner).wait_recv()
             cross_forward(k, 0).start()
             source_copy(k, 0, partner).wait_recv()
-
-            @pl.when(k > 0)
-            def _():
-                mate_copy(k, 0, other_half).wait_recv()
-
-            @pl.when(kept)
-            def _():
-                own_copy(k, 1, retiree).wait_recv()
-
-            @pl.when(moved)
-            def _():
-                own_keep(k, 1).wait()
-
-            mate_near = split(mate[k, 0])
+            mate_near = mate_high[0], mate_low[0]
             rhs = gs[k, 1 - keep] - mm(split(goth[k, 0]), mate_near)
             cross_forward(k, 0, other_half).wait_recv()
             cross_near = split(cross[k, 0])
-            coupling = mm(cross_near, mate_near)
-            y = solved(jnp.concatenate([own[k, 1], rhs], axis=0), coupling)
+            rest = inverse_rest(mm(cross_near, mate_near))
+
+            @pl.when(kept)
+            def _():
+                own_copy(k, 1, retiree).wait_recv()
+
+            @pl.when(moved)
+            def _():
+                own_keep(k, 1).wait()
+
+            rows = jnp.concatenate([own[k, 1], rhs], axis=0)
+            y = rows + mm(split(rows), split(rest))
             y_parts = split(y)
+            cross_copy(k, 1, partner).wait_recv()
+            cross_forward(k, 1).start()
             z = mm(y_parts, cross_near)
             z_own = z[:half_size]
             t = goth[k, 0] - z[half_size:]
@@ -276,28 +294,21 @@
             def _():
                 mate_send(k, 1, r["target"]).wait_recv()
                 mate_copy(k, 1).start()
-
-            @pl.when(k > 0)
-            def _():
+                own_keep(k, 0).wait()
                 mate_copy(k, 1, other_half).wait_recv()
+                split_mate(1)
 
             @pl.when(kept)
             def _():
                 own_copy(k, 0, retiree).wait_recv()
 
-            @pl.when(moved)
-            def _():
-                own_keep(k, 0).wait()
-
             near = jnp.concatenate([own[k, 0], gs[k, keep]], axis=0) + mm(
-                split(jnp.concatenate([z_own, -t], axis=0)), split(mate[k, 1])
+                split(jnp.concatenate([z_own, -t], axis=0)), (mate_high[1], mate_low[1])
             )
             side[k + 1, 0] = near[:half_size]
             gs[k + 1, 0] = near[half_size:]
             send_side(k + 1, 0, following, near[:half_size])
 
-            cross_copy(k, 1, partner).wait_recv()
-            cross_forward(k, 1).start()
             source_copy(k, 1, partner).wait_recv()
             cross_forward(k, 1, other_half).wait_recv()
             product = mm(y_parts, split(cross[k, 1]))
@@ -350,7 +361,8 @@
         cross_forward(top, 0, other_half).wait_recv()
         cross_near = split(cross[top, 0])
         coupling = mm(cross_near, mate_near)
-        t = goth[top, 0] - mm(split(solved(rhs, coupling)), cross_near)
+        middle = rhs + mm(split(rhs), split(inverse_rest(coupling)))
+        t = goth[top, 0] - mm(split(middle), cross_near)
         ebuf[top, 0] = jnp.zeros_like(t)
         esrc[top] = t
         new_edge_copy(top, 1, r_top["retiree"]).start()
@@ -494,6 +506,8 @@
             pltpu.VMEM((levels, columns, block), f32),
             pltpu.VMEM((2 * block, block), jnp.bfloat16),
             pltpu.VMEM((2 * block, block), jnp.bfloat16),
+            pltpu.VMEM((2, block, block), jnp.bfloat16),
+            pltpu.VMEM((2, block, block), jnp.bfloat16),
         ]
         + [pair] * 15
         + [one] * 6,

time: 134 us -> 132 us (0.985)
  Pallas kernels: 129 us -> 127 us
    pallas_call x1, Pallas kernels: 129 us -> 127 us  [local(): pl.pallas_call(functools.partial(kernel, levels), out_shape=jax.ShapeDtyp...]
where the time goes in v3:
time: 132 us
  Pallas kernels  127 us (96%)
  local copies, waits for them, and re-layouts  2.53 us (2%)
  matrix products  1.8 us (1%)
    pallas_call x1, Pallas kernels, local(): pl.pallas_call(functools.partial(kernel, levels), out_shape=jax.ShapeDtyp...  127 us

profile of v3, /device:TPU:30, one launch (start us, length us, event | category | flops | bytes accessed | tf_op | source)
XLA Modules:
  0.0 131.6 jit_solution(15041387231211371777)
XLA Ops:
  0.0 0.0 copy-start
  0.0 1.2 fusion.4
  1.2 0.1 copy.8
  1.3 0.1 copy.9
  1.4 0.0 copy-done
  1.5 0.1 copy.10
  1.6 0.1 copy.11
  1.8 0.0 copy-start.2
  1.8 0.1 pad_maximum_fusion.tips
  1.9 0.8 copy-done.2
  2.7 0.0 copy-start.1
  2.7 127.0 %shard_map.37 = f32[2,32,256]{2,1,0:T(8,128)S(1)} custom-call(f32[4,256,256]{2,1,0:T(8,128)S(1)} %pad_maximum_fusion.tips, f32[2,32,256]{2,1,0:T(8,128)S(1)} %pad_maximum_fusion.1.sources), custom_call_target="tpu_custom_call" | custom-call | tf_op jit(solution)/shard_map/pallas_call | solution.py:489
  129.7 0.6 convolution_subtract_fusion.1
  130.3 0.0 copy-done.1
  130.3 1.2 convolution_subtract_fusion
  (3 shorter events, 0.0 us)
Async XLA Ops:
  0.0 1.4 %copy-start = (f32[1024,256]{1,0:T(8,128)S(1)}, f32[1024,256]{1,0:T(8,128)}, u32[]{:S(2)}) copy-start(f32[1024,256]{1,0:T(8,128)} %param.3) | copy-start | bytes 3145732
  1.8 0.9 copy-start.2
  2.7 127.6 %copy-start.1 = (f32[1024,256]{1,0:T(8,128)S(1)}, f32[1024,256]{1,0:T(8,128)}, u32[]{:S(2)}) copy-start(f32[1024,256]{1,0:T(8,128)} %param.4) | copy-start | bytes 3145732

commit v4 on v3

--- a/solution.py
+++ b/solution.py
@@ -190,16 +190,21 @@
         cross_copy(0, j, first_partner).start()
         source_copy(0, j, first_partner).start()
 
-    def inverse_rest(coupling):
-        power = split(coupling)
-        rest = coupling
-        for _ in range(2):
-            square = mm(power, power)
-            power = split(square)
-            rest = rest + square + mm(split(rest), power)
-        dot = functools.partial(jnp.dot, preferred_element_type=jnp.float32)
-        last = dot(power[0], power[0])
-        return rest + last + dot(rest.astype(jnp.bfloat16), last.astype(jnp.bfloat16))
+    dot = functools.partial(jnp.dot, preferred_element_type=jnp.float32)
+
+    def approx_rest(coupling):
+        first = coupling.astype(jnp.bfloat16)
+        square = dot(first, first)
+        second = square.astype(jnp.bfloat16)
+        rest = coupling + square + dot(first, second)
+        fourth = dot(second, second)
+        rest = rest + fourth + dot(rest.astype(jnp.bfloat16), fourth.astype(jnp.bfloat16))
+        return rest.astype(jnp.bfloat16)
+
+    def refined(rows, rest, coupling):
+        start = rows + dot(rows.astype(jnp.bfloat16), rest)
+        residual = (rows - start) + mm(split(start), coupling)
+        return start + (residual + dot(residual.astype(jnp.bfloat16), rest))
 
     def send_side(k, j, r, value):
         below_top = k < top
@@ -268,7 +273,9 @@
             rhs = gs[k, 1 - keep] - mm(split(goth[k, 0]), mate_near)
             cross_forward(k, 0, other_half).wait_recv()
             cross_near = split(cross[k, 0])
-            rest = inverse_rest(mm(cross_near, mate_near))
+            coupling = mm(cross_near, mate_near)
+            rest = approx_rest(coupling)
+            coupling = split(coupling)
 
             @pl.when(kept)
             def _():
@@ -279,16 +286,13 @@
                 own_keep(k, 1).wait()
 
             rows = jnp.concatenate([own[k, 1], rhs], axis=0)
-            y = rows + mm(split(rows), split(rest))
+            y = refined(rows, rest, coupling)
             y_parts = split(y)
             cross_copy(k, 1, partner).wait_recv()
             cross_forward(k, 1).start()
             z = mm(y_parts, cross_near)
             z_own = z[:half_size]
             t = goth[k, 0] - z[half_size:]
-            trec[k] = t
-            ysrc[k] = y[:half_size]
-            zrec[k, half] = z_own
 
             @pl.when(moved)
             def _():
@@ -309,6 +313,9 @@
             gs[k + 1, 0] = near[half_size:]
             send_side(k + 1, 0, following, near[:half_size])
 
+            trec[k] = t
+            ysrc[k] = y[:half_size]
+            zrec[k, half] = z_own
             source_copy(k, 1, partner).wait_recv()
             cross_forward(k, 1, other_half).wait_recv()
             product = mm(y_parts, split(cross[k, 1]))
@@ -361,7 +368,7 @@
         cross_forward(top, 0, other_half).wait_recv()
         cross_near = split(cross[top, 0])
         coupling = mm(cross_near, mate_near)
-        middle = rhs + mm(split(rhs), split(inverse_rest(coupling)))
+        middle = refined(rhs, approx_rest(coupling), split(coupling))
         t = goth[top, 0] - mm(split(middle), cross_near)
         ebuf[top, 0] = jnp.zeros_like(t)
         esrc[top] = t
@@ -398,7 +405,6 @@
 
             own_edge = ebuf[k, 0]
             high, low = split(jnp.concatenate([own_edge, -ebuf[k, 1]], axis=1))
-            dot = functools.partial(jnp.dot, preferred_element_type=jnp.float32)
             columns = own_edge.shape[0]
             stacked = dot(jnp.concatenate([high, low], axis=0), rec_high[...])
             new = trec[k] + (

time: 132 us -> 131 us (level)
  no operation moved by 1% of the time
where the time goes in v4:
time: 131 us; the launch traced here: 130 us
  Pallas kernels  126 us (96%)
  local copies, waits for them, and re-layouts  2.53 us (2%)
  matrix products  1.8 us (1%)
    pallas_call x1, Pallas kernels, local(): pl.pallas_call(functools.partial(kernel, levels), out_shape=jax.ShapeDtyp...  126 us

profile of v4, /device:TPU:30, one launch (start us, length us, event | category | flops | bytes accessed | tf_op | source)
XLA Modules:
  0.0 130.5 jit_solution(8615079210923663569)
XLA Ops:
  0.0 0.0 copy-start
  0.0 1.2 fusion.4
  1.2 0.1 copy.8
  1.3 0.1 copy.9
  1.4 0.0 copy-done
  1.5 0.1 copy.10
  1.6 0.1 copy.11
  1.8 0.0 copy-start.2
  1.8 0.1 pad_maximum_fusion.tips
  1.9 0.8 copy-done.2
  2.7 0.0 copy-start.1
  2.7 126.0 %shard_map.37 = f32[2,32,256]{2,1,0:T(8,128)S(1)} custom-call(f32[4,256,256]{2,1,0:T(8,128)S(1)} %pad_maximum_fusion.tips, f32[2,32,256]{2,1,0:T(8,128)S(1)} %pad_maximum_fusion.1.sources), custom_call_target="tpu_custom_call" | custom-call | tf_op jit(solution)/shard_map/pallas_call | solution.py:495
  128.7 0.6 convolution_subtract_fusion.1
  129.3 0.0 copy-done.1
  129.3 1.2 convolution_subtract_fusion
  (3 shorter events, 0.0 us)
Async XLA Ops:
  0.0 1.4 %copy-start = (f32[1024,256]{1,0:T(8,128)S(1)}, f32[1024,256]{1,0:T(8,128)}, u32[]{:S(2)}) copy-start(f32[1024,256]{1,0:T(8,128)} %param.3) | copy-start | bytes 3145732
  1.8 0.9 copy-start.2
  2.7 126.6 %copy-start.1 = (f32[1024,256]{1,0:T(8,128)S(1)}, f32[1024,256]{1,0:T(8,128)}, u32[]{:S(2)}) copy-start(f32[1024,256]{1,0:T(8,128)} %param.4) | copy-start | bytes 3145732

commit v5 on v4

--- a/solution.py
+++ b/solution.py
@@ -186,8 +186,8 @@
     pl.semaphore_wait(barrier, greeted)
 
     first_partner = roles(0)["partner"]
+    cross_copy(0, 0, first_partner).start()
     for j in range(2):
-        cross_copy(0, j, first_partner).start()
         source_copy(0, j, first_partner).start()
 
     dot = functools.partial(jnp.dot, preferred_element_type=jnp.float32)
@@ -214,7 +214,8 @@
 
         @pl.when(both(active, keeps))
         def _():
-            cross_copy(k, j, r["partner"]).start()
+            if j == 0:
+                cross_copy(k, j, r["partner"]).start()
             mate[k, j, half] = value
             mate_copy(k, j).start()
             source_copy(k, j, r["partner"]).start()
@@ -268,6 +269,15 @@
 
             cross_copy(k, 0, partner).wait_recv()
             cross_forward(k, 0).start()
+
+            @pl.when(r["keeps"])
+            def _():
+                cross_copy(k, 1, partner).start()
+
+            @pl.when(k > 0)
+            def _():
+                y_copy(k - 1, roles(jnp.maximum(k - 1, 0))["partner"]).start()
+
             source_copy(k, 0, partner).wait_recv()
             mate_near = mate_high[0], mate_low[0]
             rhs = gs[k, 1 - keep] - mm(split(goth[k, 0]), mate_near)
@@ -337,7 +347,9 @@
                         mate_send(k + 1, j, following["target"]).wait_send()
                         cross_copy(k + 1, j, following["partner"]).wait_send()
 
-            y_copy(k, partner).start()
+            @pl.when(following["retiring"])
+            def _():
+                y_copy(k, partner).start()
 
         return carry
 
@@ -361,6 +373,7 @@
     def _():
         cross_copy(top, 0, r_top["partner"]).wait_recv()
         cross_forward(top, 0).start()
+        y_copy(top - 1, roles(top - 1)["partner"]).start()
         source_copy(top, 0, r_top["partner"]).wait_recv()
         mate_copy(top, 0, other_half).wait_recv()
         mate_near = split(mate[top, 0])

time: 131 us -> 150 us (1.15)
  Pallas kernels: 126 us -> 145 us
    pallas_call x1, Pallas kernels: 126 us -> 145 us  [local(): pl.pallas_call(functools.partial(kernel, levels), out_shape=jax.ShapeDtyp...]
where the time goes in v5:
time: 150 us
  Pallas kernels  145 us (97%)
  local copies, waits for them, and re-layouts  2.53 us (2%)
  matrix products  1.8 us (1%)
    pallas_call x1, Pallas kernels, local(): pl.pallas_call(functools.partial(kernel, levels), out_shape=jax.ShapeDtyp...  145 us

profile of v5, /device:TPU:30, one launch (start us, length us, event | category | flops | bytes accessed | tf_op | source)
XLA Modules:
  0.0 150.0 jit_solution(15208797616260068997)
XLA Ops:
  0.0 0.0 copy-start
  0.0 1.2 fusion.4
  1.2 0.1 copy.8
  1.3 0.1 copy.9
  1.4 0.0 copy-done
  1.5 0.1 copy.10
  1.6 0.1 copy.11
  1.8 0.0 copy-start.2
  1.8 0.1 pad_maximum_fusion.tips
  1.9 0.8 copy-done.2
  2.7 0.0 copy-start.1
  2.7 145.5 %shard_map.37 = f32[2,32,256]{2,1,0:T(8,128)S(1)} custom-call(f32[4,256,256]{2,1,0:T(8,128)S(1)} %pad_maximum_fusion.tips, f32[2,32,256]{2,1,0:T(8,128)S(1)} %pad_maximum_fusion.1.sources), custom_call_target="tpu_custom_call" | custom-call | tf_op jit(solution)/shard_map/pallas_call | solution.py:508
  148.2 0.6 convolution_subtract_fusion.1
  148.8 0.0 copy-done.1
  148.8 1.2 convolution_subtract_fusion
  (3 shorter events, 0.0 us)
Async XLA Ops:
  0.0 1.4 copy-start
  1.8 0.9 copy-start.2
  2.7 146.1 %copy-start.1 = (f32[1024,256]{1,0:T(8,128)S(1)}, f32[1024,256]{1,0:T(8,128)}, u32[]{:S(2)}) copy-start(f32[1024,256]{1,0:T(8,128)} %param.4) | copy-start | bytes 3145732
